TPU v7x, 32 devices: a whole 2x2x4 slice. The times are simulated.
32 devices in a mesh: band: 2 (over x), wide: 8 (over z, y), narrow: 2 (over core).
Axes of the slice: x: 2, y: 2, z: 4, core: 2. Of those that a mesh axis runs over, the one named last changes fastest.
Arguments:
- voltages: bfloat16 [2, 1024, 268288], P(None, ('band', 'narrow', 'wide')), parts along dimension 1, may hold values from -6 to 6
- fir_taps: float32 [4, 2048], replicated, may hold values from -0.046875 to 0.046875
- flags: int32 [1024], P(('band', 'narrow', 'wide')), parts along dimension 0, may hold values 0 or 1
- tile_order: int32 [256], replicated, may hold values from 0 to 255, each once
Outputs:
- visibilities: bfloat16 [128, 2, 512, 512], P(('band', 'wide'), None, 'narrow'), parts along dimension 0
There are 2 independent parts, one for each index of `band`. A program takes and returns all parts, laid end to end along the dimension named above; an argument that names none is the same for every part. Nothing has to cross between parts.
Inputs may be any that keep to these rules, and one draw needn't show every extreme that they name: `tile_order`: each station appears exactly once.
All inputs are finite; a program needn't handle non-finite values. No bound on the sum of `flags` on one device may be relied on, other than what follows from the above.
Results may differ from a plain program's by a relative error of at most 0.0071.
Values may be sent and summed in bfloat16 or wider, within the bound.
A program may use at most 256 MiB of HBM per device.

v0:
```python
import math

import jax
import jax.numpy as jnp
from jax import lax
from jax.sharding import PartitionSpec as P

NFFT = 2048
TAPS = 4
CH_DEV = 8


def dft_table(points, kept):
    index_n = jnp.arange(points, dtype=jnp.int32)[:, None]
    index_c = jnp.arange(kept, dtype=jnp.int32)[None, :]
    phase = index_n * index_c % points
    theta = phase.astype(jnp.float32) * (2.0 * math.pi / points)
    cosine = jnp.cos(theta)
    sine = jnp.sin(theta)
    upper = jnp.stack([cosine, -sine], -1)
    lower = jnp.stack([sine, cosine], -1)
    return jnp.concatenate([upper, lower], 0).astype(jnp.bfloat16)


def filter_bank(block, fir_taps):
    frames = block.reshape(2, block.shape[1], -1, NFFT)
    steps = frames.shape[2] - TAPS + 1
    total = jnp.zeros((2, block.shape[1], steps, NFFT), jnp.float32)
    for tap in range(TAPS):
        total = total + fir_taps[tap][None, None, None, :] * frames[
            :, :, tap : tap + steps, :
        ].astype(jnp.float32)
    return total.astype(jnp.bfloat16)


def body(voltages, fir_taps, flags, tile_order):
    local_inputs = voltages.shape[1]
    width_wide = lax.axis_size("wide")
    width_narrow = lax.axis_size("narrow")
    kept = CH_DEV * width_wide
    filtered = filter_bank(voltages, fir_taps)
    steps = filtered.shape[2]
    table = dft_table(NFFT, kept)
    spec = jnp.einsum(
        "itn,ncr->crit", filtered[0], table[:NFFT], preferred_element_type=jnp.float32
    )
    spec = spec + jnp.einsum(
        "itn,ncr->crit", filtered[1], table[NFFT:], preferred_element_type=jnp.float32
    )
    spec = spec * flags.astype(jnp.float32)[None, None, :, None]
    spectra = jnp.concatenate([spec[:, 0], spec[:, 1]], -1).astype(jnp.bfloat16)
    column_index = (2 * tile_order[:, None] + jnp.arange(2, dtype=jnp.int32)[None, :]).reshape(-1)
    paired_in = lax.all_gather(spectra, "narrow", axis=1, tiled=True)
    turned = lax.all_to_all(paired_in, "wide", split_axis=0, concat_axis=1, tiled=True)
    grouped = turned.reshape(
        turned.shape[0], width_wide, width_narrow, local_inputs, turned.shape[2]
    )
    rows_mine = lax.dynamic_slice_in_dim(grouped, lax.axis_index("narrow"), 1, 2)
    rows_mine = rows_mine.reshape(turned.shape[0], width_wide * local_inputs, turned.shape[2])
    span = width_wide * local_inputs
    narrow_part = column_index // span
    remainder = column_index % span
    wide_part = remainder // local_inputs
    local_part = remainder % local_inputs
    position = (wide_part * width_narrow + narrow_part) * local_inputs + local_part
    columns = jnp.take(turned, position, axis=1)
    rotated = jnp.concatenate([-columns[..., steps:], columns[..., :steps]], -1)
    stacked_cols = jnp.stack([columns, rotated], 1)
    tiles = jnp.einsum(
        "cim,csjm->csij", rows_mine, stacked_cols, preferred_element_type=jnp.float32
    )
    return (tiles / steps).astype(jnp.bfloat16)


def solution(mesh):
    placed = (P(None, ("band", "narrow", "wide"), None), P(), P(("band", "narrow", "wide")), P())
    return jax.shard_map(
        body,
        mesh=mesh,
        in_specs=placed,
        out_specs=P(("band", "wide"), None, "narrow", None),
        check_vma=False,
    )
```

profile of v0, /device:TPU:0, one launch (start us, length us, event | category | flops | bytes accessed | tf_op | source)
XLA Modules:
  0.0 244.0 jit_solution(13070282219535904842)
XLA Ops:
  6.5 0.0 all-gather.2.cloned.1.call-start
  6.5 2.1 cosine_convert_fusion
  8.7 2.0 negate_convert_fusion
  10.7 0.9 fusion.34
  11.6 0.0 copy-start.3
  11.6 50.5 %reshape.281 = bf16[2,32,131,2048]{3,2,1,0:T(8,128)(2,1)} reshape(bf16[2,32,268288]{2,1,0:T(8,128)(2,1)} %param.4) | data formatting | bytes 68681728 | tf_op jit(solution)/shard_map/reshape | solution.py:26
  62.2 0.0 copy-done.3
  62.2 58.9 %add_convert_fusion = bf16[2,32,128,2048]{3,2,1,0:T(8,128)(2,1)} fusion(bf16[2,32,131,2048]{3,2,1,0:T(8,128)(2,1)} %reshape.281, f32[2048]{0:T(1024)S(1)} %bitcast.60, f32[2048]{0:T(1024)S(1)} %bitcast.61, f32[2048]{0:T(1024)S(1)} %bitcast.59, f32[2048]{0:T(1024)S(1)} %bitcast.58), kind=kLoop, calls=%fused_computation.1 | loop fusion | flops 201326592 | bytes 167804928 | tf_op jit(solution)/shard_map/convert_element_type | solution.py:33
  121.0 12.7 %fusion = f32[64,2,32,128]{3,0,2,1:T(8,128)} fusion(bf16[2,32,128,2048]{3,2,1,0:T(8,128)(2,1)} %add_convert_fusion, bf16[2048,64,1]{0,1,2:T(8,128)(2,1)S(1)} %get-tuple-element.13, bf16[2048,64,1]{0,1,2:T(8,128)(2,1)S(1)} %get-tuple-element.14), kind=kOutput, calls=%fused_computation.3 | convolution fusion | flops 2148532224 | bytes 19398656 | tf_op jit(solution)/shard_map/itn,ncr->crit/dot_general | solution.py:47
  133.7 12.0 %multiply_convert_fusion.1 = bf16[64,2,32,128]{3,0,2,1:T(8,128)(2,1)S(1)} fusion(f32[64,2,32,128]{3,0,2,1:T(8,128)} %fusion, bf16[2,32,128,2048]{3,2,1,0:T(8,128)(2,1)} %add_convert_fusion, f32[32]{0:T(128)S(1)} %convert_element_type.56, bf16[2048,64,1]{0,1,2:T(8,128)(2,1)S(1)} %negate_convert_fusion, bf16[2048,64,1]{0,1,2:T(8,128)(2,1)S(1)} %get-tuple-element.13), kind=kOutput, calls=%fused_computation.16 | convolution fusion | flops 2150105088 | bytes 20447360 | tf_op jit(solution)/shard_map/itn,ncr->crit/dot_general | solution.py:44
  145.7 0.1 slice_bitcast_fusion.7
  145.8 1.1 pad_maximum_fusion
  146.9 0.0 all-gather.2.cloned.1.call-update
  147.0 0.0 copy-start.2
  147.0 13.4 %all-gather.2.cloned.1.call-done = bf16[64,64,256]{2,0,1:T(8,128)(2,1)} async-done(((bf16[64,32,256]{2,0,1:T(8,128)(2,1)}), bf16[64,64,256]{2,0,1:T(8,128)(2,1)}) %all-gather.2.cloned.1.call-update) | async-done | bytes 2097168 | tf_op jit(solution)/shard_map/all_gather | solution.py:53
  160.4 4.1 %copy.20 = bf16[64,64,256]{2,1,0:T(8,128)(2,1)} copy(bf16[64,64,256]{2,0,1:T(8,128)(2,1)} %all-gather.2.cloned.1.call-done) | data formatting | bytes 4194304 | tf_op jit(solution)/shard_map/all_gather | solution.py:53
  164.5 5.8 %all-to-all-start = ((bf16[64,64,256]{2,1,0:T(8,128)(2,1)}), bf16[64,64,256]{2,1,0:T(8,128)(2,1)S(1)}, u32[]{:S(2)}, u32[]{:S(2)}) async-start(bf16[64,64,256]{2,1,0:T(8,128)(2,1)} %copy.20), calls=%async_computation | async-start | bytes 4194304 | tf_op jit(solution)/shard_map/all_to_all | solution.py:54
  170.2 0.0 copy-done.2
  170.3 0.1 iota_add_fusion
  170.4 0.1 add.187
  170.5 0.1 add.175
  170.7 48.2 %all-to-all-done = bf16[64,64,256]{2,1,0:T(8,128)(2,1)S(1)} async-done(((bf16[64,64,256]{2,1,0:T(8,128)(2,1)}), bf16[64,64,256]{2,1,0:T(8,128)(2,1)S(1)}, u32[]{:S(2)}, u32[]{:S(2)}) %all-to-all-start) | async-done | bytes 2097184 | tf_op jit(solution)/shard_map/all_to_all | solution.py:54
  218.9 0.0 copy-start
  218.9 0.1 copy.21
  219.1 1.2 copy-done
  220.3 2.5 %copy.22 = bf16[8,512,256]{2,0,1:T(8,128)(2,1)} copy(bf16[8,512,256]{2,1,0:T(8,128)(2,1)S(1)} %bitcast.56) | data formatting | bytes 4194304 | tf_op jit(solution)/shard_map/all_to_all | solution.py:54
  222.8 2.6 %gather_fusion = bf16[512,8,256]{2,1,0:T(8,128)(2,1)S(1)} fusion(bf16[8,512,256]{2,0,1:T(8,128)(2,1)} %copy.22, s32[1024]{0:T(1024)S(1)} %pad_clamp_fusion), kind=kCustom, calls=%fused_computation | custom fusion | bytes 4196352 | tf_op jit(solution)/shard_map/jit(_take)/gather | solution.py:66
  225.4 0.5 bitcast_select_fusion.1
  225.8 0.0 copy-start.1
  225.8 0.5 fusion.9
  226.3 0.2 slice_negate_fusion
  226.6 0.9 copy-done.1
  227.4 0.1 constant_dynamic-slice_fusion
  227.5 0.1 copy.30
  227.6 0.2 maximum_bitcast_fusion
  227.9 2.8 %fusion.2 = bf16[8,2,256,512]{2,3,1,0:T(8,128)(2,1)} fusion(bf16[8,256,256,1]{2,1,3,0:T(8,128)(2,1)S(1)} %bitcast.57, bf16[8,1,512,256]{3,2,1,0:T(8,128)(2,1)S(1)} %maximum_bitcast_fusion, bf16[8,1,512,256]{3,2,1,0:T(8,128)(2,1)S(1)} %fusion.9), kind=kOutput, calls=%fused_computation.7 | convolution fusion | flops 1080033280 | bytes 9437184 | tf_op jit(solution)/shard_map/cim,csjm->csij/dot_general | solution.py:69
  230.7 6.4 %copy.26 = bf16[8,2,256,512]{3,2,1,0:T(8,128)(2,1)} copy(bf16[8,2,256,512]{2,3,1,0:T(8,128)(2,1)} %fusion.2) | data formatting | bytes 8388608 | tf_op jit(solution)/shard_map/convert_element_type | solution.py:72
  (5 shorter events, 0.1 us)
Async XLA Ops:
  6.5 153.8 %all-gather.2.cloned.1.call-start = ((), (), s32[]{:S(2)}) async-start(), calls=%async_computation.1 | async-start | bytes 3145728 | tf_op jit(solution)/shard_map/all_gather | solution.py:53
  11.6 50.5 %copy-start.3 = (s32[32]{0:T(128)S(1)}, s32[32]{0:T(128)}, u32[]{:S(2)}) copy-start(s32[32]{0:T(128)} %param.6) | copy-start | bytes 388
  147.0 23.3 %copy-start.2 = (s32[256]{0:T(256)S(1)}, s32[256]{0:T(256)}, u32[]{:S(2)}) copy-start(s32[256]{0:T(256)} %param.7) | copy-start | bytes 3076
  164.5 54.5 %all-to-all-start = ((bf16[64,64,256]{2,1,0:T(8,128)(2,1)}), bf16[64,64,256]{2,1,0:T(8,128)(2,1)S(1)}, u32[]{:S(2)}, u32[]{:S(2)}) async-start(bf16[64,64,256]{2,1,0:T(8,128)(2,1)} %copy.20), calls=%async_computation | async-start | bytes 4194304 | tf_op jit(solution)/shard_map/all_to_all | solution.py:54
  218.9 1.3 copy-start
  225.8 1.6 copy-start.1
Sparse Core Ops, SparseCore 0:
  147.1 13.2 all-gather.1
where the time goes:
time: 245 us; the launch traced here: 244 us
  local copies, waits for them, and re-layouts  69.8 us (28%)
  other arithmetic  65.7 us (27%)
  waiting for transfers between devices  61.6 us (25%)
  matrix products  27.6 us (11%)
  between operations  13.6 us (6%)
  starting transfers between devices  5.78 us (2%)
    convert_element_type x1, other arithmetic, filter_bank(): return total.astype(jnp.bfloat16)  58.9 us
    reshape x1, local copies, waits for them, and re-layouts, filter_bank(): frames = block.reshape(2, block.shape[1], -1, NFFT)  50.5 us
    all_to_all x1, waiting for transfers between devices, body(): lax.all_to_all(paired_in, 'wide', split_axis=0, concat_axis=1, tiled=True)  48.2 us
    all_gather x1, waiting for transfers between devices, body(): paired_in = lax.all_gather(spectra, 'narrow', axis=1, tiled=True)  13.4 us
    dot_general x1, matrix products, body(): jnp.einsum('itn,ncr->crit', filtered[1], table[NFFT:], preferred_element_...  12.7 us
    dot_general x1, matrix products, body(): jnp.einsum('itn,ncr->crit', filtered[0], table[:NFFT], preferred_element_...  12 us
    convert_element_type x1, local copies, waits for them, and re-layouts, body(): return (tiles / steps).astype(jnp.bfloat16)  6.44 us
    all_to_all x1, starting transfers between devices, body(): lax.all_to_all(paired_in, 'wide', split_axis=0, concat_axis=1, tiled=True)  5.77 us
  transfers between devices with their start and end apart: 2, of which 2 were waited for; matrix products, arithmetic and copies ran while one was open for 0% of the time, Pallas kernels for 0%

commit v1 on v0

v1 whole, which is shorter than its diff:
```python
import functools
import math

import jax
import jax.numpy as jnp
import ml_dtypes
import numpy as np
from jax import lax
from jax.experimental import pallas as pl
from jax.experimental.pallas import tpu as pltpu
from jax.sharding import PartitionSpec as P

NFFT = 2048
TAPS = 4
CH_DEV = 8
HALF = 64
MESH = pl.DeviceIdType.MESH


def dft_table(points, kept):
    phase = np.arange(points)[:, None] * np.arange(kept)[None, :] % points
    theta = phase * (2.0 * math.pi / points)
    cosine, sine = np.cos(theta), np.sin(theta)
    upper = np.concatenate([cosine, -sine], 1)
    lower = np.concatenate([sine, cosine], 1)
    return np.concatenate([upper, lower], 0).astype(ml_dtypes.bfloat16)


def channelise(wide, nq, rows, halves, volt, dft, fir, flags, out, frames, table, grid_sum, spec,
               stage, send, in_sem, send_sem, recv_sem, own_sem, fwd_send, fwd_recv):
    me = lax.axis_index("wide")
    core = lax.axis_index("narrow")
    kept = CH_DEV * wide
    span = 2 * kept
    steps = HALF + TAPS - 1
    chunks = nq * halves

    def load(chunk):
        q, th = chunk // halves, chunk % halves

        @pl.loop(0, steps)
        def _(s):
            for part in range(2):
                pltpu.make_async_copy(
                    volt.at[part, pl.ds(q * rows, rows), pl.ds(pl.multiple_of((th * HALF + s) * NFFT, NFFT), NFFT)],
                    frames.at[chunk, s, :, pl.ds(part * NFFT, NFFT)],
                    in_sem.at[chunk],
                ).start()

    for chunk in range(chunks):
        load(chunk)

    barrier = pltpu.get_barrier_semaphore()
    for d in range(1, wide):
        pl.semaphore_signal(barrier, inc=1, device_id={"wide": lax.rem(me + d, wide)}, device_id_type=MESH)
    pl.semaphore_signal(barrier, inc=1, device_id={"narrow": 1 - core}, device_id_type=MESH)

    taps = jnp.concatenate([fir[...], fir[...]], 0).T
    step_n = 256
    for n0 in range(0, NFFT, step_n):
        for part in range(2):
            base = part * NFFT + n0
            w = dft[base : base + step_n, :].astype(jnp.float32)
            for k in range(TAPS):
                table[base : base + step_n, k * span : (k + 1) * span] = (
                    w * taps[n0 : n0 + step_n, k : k + 1]
                ).astype(jnp.bfloat16)

    pl.semaphore_wait(barrier, wide)

    def place(chunk, source):
        q, th = chunk // halves, chunk % halves
        return out.at[th, :, (core * wide + source) * nq + q]

    def to_peer(chunk, peer):
        return pltpu.make_async_remote_copy(
            src_ref=send.at[chunk, pl.ds(peer * CH_DEV, CH_DEV)],
            dst_ref=place(chunk, me),
            send_sem=send_sem,
            recv_sem=recv_sem.at[chunk, me],
            device_id={"wide": peer},
            device_id_type=MESH,
        )

    @pl.loop(0, chunks)
    def _(chunk):
        pltpu.make_async_copy(frames.at[chunk], frames.at[chunk], in_sem.at[chunk]).wait()
        lhs = frames[chunk]
        if rows % 16:
            lhs = lhs.astype(jnp.float32).reshape(steps * rows, 2 * NFFT).astype(jnp.bfloat16)
        else:
            lhs = lhs.reshape(steps * rows, 2 * NFFT)
        grid_sum[...] = jnp.dot(lhs, table[...], preferred_element_type=jnp.float32)
        count = HALF * rows
        total = grid_sum[0:count, 0:span]
        for k in range(1, TAPS):
            total = total + grid_sum[k * rows : k * rows + count, k * span : (k + 1) * span]
        for lane in range(0, span, 128):
            spec[lane // 128] = total[:, lane : lane + 128]
        q = chunk // halves
        for i in range(rows):
            pieces = [spec[b, pl.ds(i, HALF, stride=rows), :] for b in range(span // 128)]
            if kept % 128:
                piece = pieces[0]
                both = jnp.concatenate([piece, pltpu.roll(piece, kept, 1)], 0).T[:kept]
            else:
                mid = kept // 128
                both = jnp.concatenate(
                    [jnp.concatenate([pieces[b], pieces[mid + b]], 0).T for b in range(mid)], 0
                )
            both = both * flags[q * rows + i].astype(jnp.float32)
            stage[pl.ds(i, kept, stride=rows), :] = both
        send[chunk] = stage[...].reshape(kept, rows, 2 * HALF).astype(jnp.bfloat16)
        for d in range(1, wide):
            to_peer(chunk, lax.rem(me + d, wide)).start()
        pltpu.make_async_copy(
            send.at[chunk, pl.ds(me * CH_DEV, CH_DEV)], place(chunk, me), own_sem
        ).start()
        pltpu.make_async_remote_copy(
            src_ref=send.at[chunk, pl.ds(me * CH_DEV, CH_DEV)],
            dst_ref=place(chunk, me),
            send_sem=fwd_send,
            recv_sem=fwd_recv,
            device_id={"narrow": 1 - core},
            device_id_type=MESH,
        ).start()

    @pl.loop(0, chunks)
    def _(chunk):
        for d in range(1, wide):
            source = lax.rem(me + wide - d, wide)
            here = place(chunk, source)
            pltpu.make_async_copy(here, here, recv_sem.at[chunk, source]).wait()
            pltpu.make_async_remote_copy(
                src_ref=here,
                dst_ref=here,
                send_sem=fwd_send,
                recv_sem=fwd_recv,
                device_id={"narrow": 1 - core},
                device_id_type=MESH,
            ).start()

    half_out = out.at[:, :, pl.ds(0, wide * nq)]
    pltpu.make_async_copy(half_out, half_out, fwd_send).wait()
    pltpu.make_async_copy(half_out, half_out, fwd_recv).wait()
    sent = send.at[:, pl.ds(0, (wide - 1) * CH_DEV)]
    pltpu.make_async_copy(sent, sent, send_sem).wait()
    own = send.at[:, pl.ds(0, CH_DEV)]
    pltpu.make_async_copy(own, own, own_sem).wait()


def correlate(halves, order, spectra, out, pick):
    inputs = pick.shape[0]
    local = inputs // 2
    core = lax.axis_index("narrow")

    @pl.when(pl.program_id(0) == 0)
    def _():
        stations = inputs // 2
        spread = (
            lax.broadcasted_iota(jnp.int32, (stations, inputs), 0)
            == lax.broadcasted_iota(jnp.int32, (stations, inputs), 1) // 2
        ).astype(jnp.float32).astype(jnp.bfloat16)
        row = jnp.broadcast_to(order[...].astype(jnp.float32), (16, stations)).astype(jnp.bfloat16)
        wide_row = jnp.dot(row, spread, preferred_element_type=jnp.float32)[0:1]
        odd = lax.broadcasted_iota(jnp.int32, (1, inputs), 1) % 2
        column = 2 * wide_row.astype(jnp.int32) + odd
        hit = lax.broadcasted_iota(jnp.int32, (inputs, inputs), 0) == column
        pick[...] = hit.astype(jnp.float32).T.astype(jnp.bfloat16)

    lane = lax.broadcasted_iota(jnp.int32, (inputs, 2 * HALF), 1)
    sign = jnp.where(lane < HALF, -1.0, 1.0)
    rows, cols, turned = [], [], []
    for th in range(halves):
        block = spectra[th, 0]
        if block.shape[1] % 16:
            block = block.astype(jnp.float32).reshape(inputs, 2 * HALF).astype(jnp.bfloat16)
        else:
            block = block.reshape(inputs, 2 * HALF)
        rows.append(jnp.where(core == 0, block[:local], block[local:]))
        picked = jnp.dot(pick[...], block, preferred_element_type=jnp.float32)
        cols.append(picked.astype(jnp.bfloat16))
        turned.append((pltpu.roll(picked, HALF, 1) * sign).astype(jnp.bfloat16))
    left = jnp.concatenate(rows, 1)
    contract = (((1,), (1,)), ((), ()))
    for part, right in enumerate((cols, turned)):
        tile = lax.dot_general(
            left, jnp.concatenate(right, 1), contract, preferred_element_type=jnp.float32
        )
        out[0, part] = (tile * (1.0 / (halves * HALF))).astype(jnp.bfloat16)


def body(voltages, fir_taps, flags, tile_order):
    local_inputs, samples = voltages.shape[1:]
    wide = lax.axis_size("wide")
    narrow = lax.axis_size("narrow")
    times = samples // NFFT - TAPS + 1
    halves = times // HALF
    rows = 16 if local_inputs % 16 == 0 else local_inputs
    nq = local_inputs // rows
    chunks = nq * halves
    kept = CH_DEV * wide
    span = 2 * kept
    steps = HALF + TAPS - 1
    groups = narrow * wide * nq
    inputs = groups * rows
    vmem = pl.BlockSpec(memory_space=pltpu.VMEM)
    hbm = pl.BlockSpec(memory_space=pl.ANY)
    spectra = pl.pallas_call(
        functools.partial(channelise, wide, nq, rows, halves),
        out_shape=jax.ShapeDtypeStruct((halves, CH_DEV, groups, rows, 2 * HALF), jnp.bfloat16),
        in_specs=[hbm, vmem, vmem, pl.BlockSpec(memory_space=pltpu.SMEM)],
        out_specs=hbm,
        scratch_shapes=[
            pltpu.VMEM((chunks, steps, rows, 2 * NFFT), jnp.bfloat16),
            pltpu.VMEM((2 * NFFT, TAPS * span), jnp.bfloat16),
            pltpu.VMEM((steps * rows, TAPS * span), jnp.float32),
            pltpu.VMEM((span // 128, HALF * rows, 128), jnp.float32),
            pltpu.VMEM((kept * rows, 2 * HALF), jnp.float32),
            pltpu.VMEM((chunks, kept, rows, 2 * HALF), jnp.bfloat16),
            pltpu.SemaphoreType.DMA((chunks,)),
            pltpu.SemaphoreType.DMA,
            pltpu.SemaphoreType.DMA((chunks, wide)),
            pltpu.SemaphoreType.DMA,
            pltpu.SemaphoreType.DMA,
            pltpu.SemaphoreType.DMA,
        ],
        compiler_params=pltpu.CompilerParams(
            collective_id=0, has_side_effects=True, vmem_limit_bytes=60 * 1024 * 1024
        ),
        cost_estimate=pl.CostEstimate(
            flops=2 * chunks * steps * rows * 2 * NFFT * TAPS * span,
            bytes_accessed=voltages.size * 2,
            transcendentals=0,
        ),
        name="channelise",
    )(voltages, jnp.asarray(dft_table(NFFT, kept)), fir_taps, flags)
    return pl.pallas_call(
        functools.partial(correlate, halves),
        grid=(CH_DEV,),
        out_shape=jax.ShapeDtypeStruct((CH_DEV, 2, inputs // narrow, inputs), jnp.bfloat16),
        in_specs=[
            pl.BlockSpec((1, tile_order.shape[0]), lambda c: (0, 0)),
            pl.BlockSpec((halves, 1, groups, rows, 2 * HALF), lambda c: (0, c, 0, 0, 0)),
        ],
        out_specs=pl.BlockSpec((1, 2, inputs // narrow, inputs), lambda c: (c, 0, 0, 0)),
        scratch_shapes=[pltpu.VMEM((inputs, inputs), jnp.bfloat16)],
        compiler_params=pltpu.CompilerParams(vmem_limit_bytes=32 * 1024 * 1024),
        cost_estimate=pl.CostEstimate(
            flops=4 * CH_DEV * inputs * inputs * 2 * HALF * halves,
            bytes_accessed=3 * CH_DEV * inputs * inputs,
            transcendentals=0,
        ),
        name="correlate",
    )(tile_order.reshape(1, -1), spectra)


def solution(mesh):
    placed = (P(None, ("band", "narrow", "wide"), None), P(), P(("band", "narrow", "wide")), P())
    return jax.shard_map(
        body,
        mesh=mesh,
        in_specs=placed,
        out_specs=P(("band", "wide"), None, "narrow", None),
        check_vma=False,
    )
```

time: 245 us -> 48.2 us (0.20)
  local copies, waits for them, and re-layouts: 69.8 us -> 1.59 us
  other arithmetic: 65.7 us -> 0 us
  waiting for transfers between devices: 61.6 us -> 0 us
  Pallas kernels: 0 us -> 46.4 us
  matrix products: 27.6 us -> 0 us
  between operations: 13.6 us -> 0.03 us
  starting transfers between devices: 5.78 us -> 0 us
    convert_element_type x2 -> x0, other arithmetic: 58.9 us -> none  [the longest x1 58.9 us: filter_bank(): return total.astype(jnp.bfloat16)]
    reshape x1 -> x0, local copies, waits for them, and re-layouts: 50.5 us -> none  [filter_bank(): frames = block.reshape(2, block.shape[1], -1, NFFT)]
    all_to_all x1 -> x0, waiting for transfers between devices: 48.2 us -> none  [body(): lax.all_to_all(paired_in, 'wide', split_axis=0, concat_axis=1, tiled=True)]
    pallas_call x0 -> x2, Pallas kernels: none -> 46.4 us  [the longest x1 39.3 us: body(): pl.pallas_call(functools.partial(channelise, wide, nq, rows, halves), out...]
    dot_general x3 -> x0, matrix products: 27.6 us -> none  [the longest x1 12.7 us: body(): jnp.einsum('itn,ncr->crit', filtered[1], table[NFFT:], preferred_element_...]
    all_gather x1 -> x0, waiting for transfers between devices: 13.4 us -> none  [body(): paired_in = lax.all_gather(spectra, 'narrow', axis=1, tiled=True)]
    convert_element_type x1 -> x0, local copies, waits for them, and re-layouts: 6.44 us -> none  [body(): return (tiles / steps).astype(jnp.bfloat16)]
    all_to_all x1 -> x0, starting transfers between devices: 5.77 us -> none  [body(): lax.all_to_all(paired_in, 'wide', split_axis=0, concat_axis=1, tiled=True)]
  transfers between devices with their start and end apart: 2 -> 0, of which waited for: 2 -> 0; matrix products, arithmetic and copies ran while one was open for 0% -> 0% of each run, Pallas kernels for 0% -> 0%
where the time goes in v1:
time: 48.2 us; the launch traced here: 48.1 us
  Pallas kernels  46.4 us (96%)
  local copies, waits for them, and re-layouts  1.59 us (3%)
    pallas_call x1, Pallas kernels, body(): pl.pallas_call(functools.partial(channelise, wide, nq, rows, halves), out...  39.3 us
    pallas_call x1, Pallas kernels, body(): pl.pallas_call(functools.partial(correlate, halves), grid=(CH_DEV,), out_...  7.2 us
    unnamed x4, local copies, waits for them, and re-layouts  1.59 us

profile of v1, /device:TPU:0, one launch (start us, length us, event | category | flops | bytes accessed | tf_op | source)
XLA Modules:
  0.0 48.1 jit_solution(17832001433194020281)
XLA Ops:
  0.0 0.0 copy-start
  0.0 39.3 %channelise.1.spectra = bf16[2,8,32,16,128]{4,3,2,1,0:T(8,128)(2,1)} custom-call(bf16[2,32,268288]{2,1,0:T(8,128)(2,1)} %volt.1, bf16[4096,128]{1,0:T(8,128)(2,1)} %constant.2.clone.dft, f32[4,2048]{1,0:T(4,128)} %fir.1, s32[32]{0:T(128)} %flags.1), custom_call_target="tpu_custom_call" | custom-call | flops 17985175552 | bytes 34340864 | tf_op jit(solution)/shard_map/channelise/pallas_call | solution.py:209
  39.3 0.0 copy-done
  39.3 0.0 copy-start.1
  39.3 1.6 %copy-done.1 = bf16[2,8,32,16,128]{4,3,2,1,0:T(8,128)(2,1)S(1)} copy-done((bf16[2,8,32,16,128]{4,3,2,1,0:T(8,128)(2,1)S(1)}, bf16[2,8,32,16,128]{4,3,2,1,0:T(8,128)(2,1)}, u32[]{:S(2)}) %copy-start.1) | copy-done | bytes 2097176
  40.9 7.2 %correlate.1 = bf16[8,2,256,512]{3,2,1,0:T(8,128)(2,1)} custom-call(s32[1,256]{1,0:T(1,128)S(1)} %bitcast.1, bf16[2,8,32,16,128]{4,3,2,1,0:T(8,128)(2,1)S(1)} %copy-done.1), custom_call_target="tpu_custom_call" | custom-call | flops 2147483648 | bytes 6291456 | tf_op jit(solution)/shard_map/correlate/pallas_call | solution.py:238
Async XLA Ops:
  0.0 39.3 %copy-start = (s32[256]{0:T(256)S(1)}, s32[256]{0:T(256)}, u32[]{:S(2)}) copy-start(s32[256]{0:T(256)} %param.8) | copy-start | bytes 3076
  39.3 1.6 %copy-start.1 = (bf16[2,8,32,16,128]{4,3,2,1,0:T(8,128)(2,1)S(1)}, bf16[2,8,32,16,128]{4,3,2,1,0:T(8,128)(2,1)}, u32[]{:S(2)}) copy-start(bf16[2,8,32,16,128]{4,3,2,1,0:T(8,128)(2,1)} %channelise.1.spectra) | copy-start | bytes 6291460

commit v2 on v1

v2 whole, which is shorter than its diff:
```python
import functools
import math

import jax
import jax.numpy as jnp
import ml_dtypes
import numpy as np
from jax import lax
from jax.experimental import pallas as pl
from jax.experimental.pallas import tpu as pltpu
from jax.sharding import PartitionSpec as P

NFFT = 2048
TAPS = 4
CH_DEV = 8
HALF = 64
MESH = pl.DeviceIdType.MESH


def dft_table(points, kept):
    phase = np.arange(points)[:, None] * np.arange(kept)[None, :] % points
    theta = phase * (2.0 * math.pi / points)
    cosine, sine = np.cos(theta), np.sin(theta)
    halves = []
    for h in range(2):
        mine = slice(h * kept // 2, (h + 1) * kept // 2)
        c, s = cosine[:, mine], sine[:, mine]
        both = np.concatenate([np.concatenate([c, -s], 1), np.concatenate([s, c], 1)], 0)
        halves.append(np.concatenate([both] * max(1, 128 // kept), 1))
    return np.stack(halves).astype(ml_dtypes.bfloat16)


def one_hot(order, inputs):
    stations = inputs // 2
    spread = (
        lax.broadcasted_iota(jnp.int32, (stations, inputs), 0)
        == lax.broadcasted_iota(jnp.int32, (stations, inputs), 1) // 2
    ).astype(jnp.float32).astype(jnp.bfloat16)
    row = jnp.broadcast_to(order.astype(jnp.float32), (16, stations)).astype(jnp.bfloat16)
    wide_row = jnp.dot(row, spread, preferred_element_type=jnp.float32)[0:1]
    odd = lax.broadcasted_iota(jnp.int32, (1, inputs), 1) % 2
    column = 2 * wide_row.astype(jnp.int32) + odd
    hit = lax.broadcasted_iota(jnp.int32, (inputs, inputs), 0) == column
    return hit.astype(jnp.float32).T.astype(jnp.bfloat16)


def channelise(wide, nq, rows, halves, volt, dft, fir, flags, order, out, pick, frames, weights,
               table, grid_sum, spec, stage, send, in_sem, dft_sem, send_sem, recv_sem, own_sem,
               fwd_send, fwd_recv):
    me = lax.axis_index("wide")
    core = lax.axis_index("narrow")
    side = me // (wide // 2)
    group = wide // 2
    kept = CH_DEV * wide
    half = kept // 2
    steps = HALF + TAPS - 1
    chunks = nq * halves
    lanes = weights.shape[1]
    fold = lanes // kept

    def weights_copy(turn):
        which = 1 - side if turn == 0 else side
        return pltpu.make_async_copy(dft.at[which], weights, dft_sem.at[turn])

    barrier = pltpu.get_barrier_semaphore()
    for d in range(1, wide):
        pl.semaphore_signal(barrier, inc=1, device_id={"wide": lax.rem(me + d, wide)}, device_id_type=MESH)
    pl.semaphore_signal(barrier, inc=1, device_id={"narrow": 1 - core}, device_id_type=MESH)

    weights_copy(0).start()

    def load(chunk):
        q, th = chunk // halves, chunk % halves

        @pl.loop(0, steps)
        def _(s):
            for part in range(2):
                pltpu.make_async_copy(
                    volt.at[part, pl.ds(q * rows, rows), pl.ds(pl.multiple_of((th * HALF + s) * NFFT, NFFT), NFFT)],
                    frames.at[chunk, s, :, pl.ds(part * NFFT, NFFT)],
                    in_sem.at[chunk],
                ).start()

    for chunk in range(chunks):
        load(chunk)

    def build():
        taps = jnp.concatenate([fir[...], fir[...]], 0).T
        step_n = 256
        lane = lax.broadcasted_iota(jnp.int32, (step_n, lanes), 1)
        for n0 in range(0, NFFT, step_n):
            scales = []
            for k in range(0, TAPS, fold):
                scale = jnp.broadcast_to(taps[n0 : n0 + step_n, k : k + 1], (step_n, lanes))
                for f in range(1, fold):
                    scale = jnp.where(lane < f * kept, scale, taps[n0 : n0 + step_n, k + f : k + f + 1])
                scales.append(scale)
            for part in range(2):
                base = part * NFFT + n0
                w = weights[base : base + step_n, :].astype(jnp.float32)
                for b, scale in enumerate(scales):
                    table[base : base + step_n, b * lanes : (b + 1) * lanes] = (w * scale).astype(jnp.bfloat16)

    def place(chunk, source):
        q, th = chunk // halves, chunk % halves
        return out.at[th, :, (core * wide + source) * nq + q]

    def to_peer(turn, chunk, peer):
        return pltpu.make_async_remote_copy(
            src_ref=send.at[turn, chunk, pl.ds(lax.rem(peer, group) * CH_DEV, CH_DEV)],
            dst_ref=place(chunk, me),
            send_sem=send_sem.at[turn],
            recv_sem=recv_sem.at[chunk, me],
            device_id={"wide": peer},
            device_id_type=MESH,
        )

    def work(turn, chunk):
        lhs = frames[chunk]
        if rows % 16:
            lhs = lhs.astype(jnp.float32).reshape(steps * rows, 2 * NFFT).astype(jnp.bfloat16)
        else:
            lhs = lhs.reshape(steps * rows, 2 * NFFT)
        grid_sum[...] = jnp.dot(lhs, table[...], preferred_element_type=jnp.float32)
        count = HALF * rows

        def tap(b, extra):
            first = b * fold * rows
            return grid_sum[first : first + count + extra * rows, b * lanes : (b + 1) * lanes]

        extra = fold - 1
        total = tap(0, extra)
        for b in range(1, TAPS // fold):
            total = total + tap(b, extra)
        if fold == 2:
            total = total[:count] + pltpu.roll(total[rows:], kept, 1)
        for b in range(lanes // 128):
            spec[b] = total[:, b * 128 : (b + 1) * 128]
        q = chunk // halves
        for i in range(rows):
            pieces = [spec[b, pl.ds(i, HALF, stride=rows), :] for b in range(lanes // 128)]
            if half % 128:
                piece = pieces[0]
                both = jnp.concatenate([piece, pltpu.roll(piece, 128 - half, 1)], 0).T[:half]
            else:
                mid = half // 128
                both = jnp.concatenate(
                    [jnp.concatenate([pieces[b], pieces[mid + b]], 0).T for b in range(mid)], 0
                )
            both = both * flags[q * rows + i].astype(jnp.float32)
            stage[pl.ds(i, half, stride=rows), :] = both
        send[turn, chunk] = stage[...].reshape(half, rows, 2 * HALF).astype(jnp.bfloat16)

    weights_copy(0).wait()
    build()
    weights_copy(1).start()
    pl.semaphore_wait(barrier, wide)

    @pl.loop(0, chunks)
    def _(chunk):
        pltpu.make_async_copy(frames.at[chunk], frames.at[chunk], in_sem.at[chunk]).wait()
        work(0, chunk)
        for d in range(group, wide):
            to_peer(0, chunk, me ^ d).start()

    weights_copy(1).wait()
    build()

    @pl.loop(0, chunks)
    def _(chunk):
        work(1, chunk)
        for d in range(1, group):
            to_peer(1, chunk, me ^ d).start()
        own = send.at[1, chunk, pl.ds(lax.rem(me, group) * CH_DEV, CH_DEV)]
        pltpu.make_async_copy(own, place(chunk, me), own_sem).start()
        pltpu.make_async_remote_copy(
            src_ref=own,
            dst_ref=place(chunk, me),
            send_sem=fwd_send,
            recv_sem=fwd_recv,
            device_id={"narrow": 1 - core},
            device_id_type=MESH,
        ).start()

    pick[...] = one_hot(order[...], pick.shape[0])

    def forward(chunk, d):
        source = me ^ d
        here = place(chunk, source)
        pltpu.make_async_copy(here, here, recv_sem.at[chunk, source]).wait()
        pltpu.make_async_remote_copy(
            src_ref=here,
            dst_ref=here,
            send_sem=fwd_send,
            recv_sem=fwd_recv,
            device_id={"narrow": 1 - core},
            device_id_type=MESH,
        ).start()

    def forward_all(low, high, first, last):
        @pl.loop(first, last)
        def _(chunk):
            for d in range(low, high):
                forward(chunk, d)

    forward_all(group, wide, 0, chunks - 1)
    forward_all(1, group, 0, chunks)
    forward_all(group, wide, chunks - 1, chunks)

    half_out = out.at[:, :, pl.ds(0, wide * nq)]
    pltpu.make_async_copy(half_out, half_out, fwd_send).wait()
    pltpu.make_async_copy(half_out, half_out, fwd_recv).wait()
    pltpu.make_async_copy(send.at[0], send.at[0], send_sem.at[0]).wait()
    if group > 1:
        sent = send.at[1, :, pl.ds(0, (group - 1) * CH_DEV)]
        pltpu.make_async_copy(sent, sent, send_sem.at[1]).wait()
    own = send.at[1, :, pl.ds(0, CH_DEV)]
    pltpu.make_async_copy(own, own, own_sem).wait()


def flat(block):
    count = block.shape[0] * block.shape[1]
    if block.shape[1] % 16:
        return block.astype(jnp.float32).reshape(count, 2 * HALF).astype(jnp.bfloat16)
    return block.reshape(count, 2 * HALF)


def correlate(halves, pick, spectra, out):
    inputs = pick.shape[0]
    mine = spectra.shape[2] // 2
    core = lax.axis_index("narrow")
    lane = lax.broadcasted_iota(jnp.int32, (inputs, 2 * HALF), 1)
    sign = jnp.where(lane < HALF, -1.0, 1.0)
    rows, cols, turned = [], [], []
    for th in range(halves):
        block = flat(spectra[th, 0])
        rows.append(flat(spectra[th, 0, pl.ds(core * mine, mine)]))
        picked = jnp.dot(pick[...], block, preferred_element_type=jnp.float32)
        cols.append(picked.astype(jnp.bfloat16))
        turned.append((pltpu.roll(picked, HALF, 1) * sign).astype(jnp.bfloat16))
    left = jnp.concatenate(rows, 1)
    contract = (((1,), (1,)), ((), ()))
    for part, right in enumerate((cols, turned)):
        tile = lax.dot_general(
            left, jnp.concatenate(right, 1), contract, preferred_element_type=jnp.float32
        )
        out[0, part] = (tile * (1.0 / (halves * HALF))).astype(jnp.bfloat16)


def body(voltages, fir_taps, flags, tile_order):
    local_inputs, samples = voltages.shape[1:]
    wide = lax.axis_size("wide")
    narrow = lax.axis_size("narrow")
    times = samples // NFFT - TAPS + 1
    halves = times // HALF
    rows = 16 if local_inputs % 16 == 0 else local_inputs
    nq = local_inputs // rows
    chunks = nq * halves
    kept = CH_DEV * wide
    steps = HALF + TAPS - 1
    groups = narrow * wide * nq
    inputs = groups * rows
    lanes = max(kept, 128)
    vmem = pl.BlockSpec(memory_space=pltpu.VMEM)
    hbm = pl.BlockSpec(memory_space=pl.ANY)
    spectra, pick = pl.pallas_call(
        functools.partial(channelise, wide, nq, rows, halves),
        out_shape=(
            jax.ShapeDtypeStruct((halves, CH_DEV, groups, rows, 2 * HALF), jnp.bfloat16),
            jax.ShapeDtypeStruct((inputs, inputs), jnp.bfloat16),
        ),
        in_specs=[hbm, hbm, vmem, pl.BlockSpec(memory_space=pltpu.SMEM), vmem],
        out_specs=(hbm, vmem),
        scratch_shapes=[
            pltpu.VMEM((chunks, steps, rows, 2 * NFFT), jnp.bfloat16),
            pltpu.VMEM((2 * NFFT, lanes), jnp.bfloat16),
            pltpu.VMEM((2 * NFFT, TAPS * kept), jnp.bfloat16),
            pltpu.VMEM((steps * rows, TAPS * kept), jnp.float32),
            pltpu.VMEM((lanes // 128, HALF * rows, 128), jnp.float32),
            pltpu.VMEM((kept // 2 * rows, 2 * HALF), jnp.float32),
            pltpu.VMEM((2, chunks, kept // 2, rows, 2 * HALF), jnp.bfloat16),
            pltpu.SemaphoreType.DMA((chunks,)),
            pltpu.SemaphoreType.DMA((2,)),
            pltpu.SemaphoreType.DMA((2,)),
            pltpu.SemaphoreType.DMA((chunks, wide)),
            pltpu.SemaphoreType.DMA,
            pltpu.SemaphoreType.DMA,
            pltpu.SemaphoreType.DMA,
        ],
        compiler_params=pltpu.CompilerParams(
            collective_id=0, has_side_effects=True, vmem_limit_bytes=60 * 1024 * 1024
        ),
        cost_estimate=pl.CostEstimate(
            flops=4 * chunks * steps * rows * 2 * NFFT * TAPS * kept,
            bytes_accessed=voltages.size * 2,
            transcendentals=0,
        ),
        name="channelise",
    )(voltages, jnp.asarray(dft_table(NFFT, kept)), fir_taps, flags, tile_order.reshape(1, -1))
    return pl.pallas_call(
        functools.partial(correlate, halves),
        grid=(CH_DEV,),
        out_shape=jax.ShapeDtypeStruct((CH_DEV, 2, inputs // narrow, inputs), jnp.bfloat16),
        in_specs=[
            pl.BlockSpec((inputs, inputs), lambda c: (0, 0)),
            pl.BlockSpec((halves, 1, groups, rows, 2 * HALF), lambda c: (0, c, 0, 0, 0)),
        ],
        out_specs=pl.BlockSpec((1, 2, inputs // narrow, inputs), lambda c: (c, 0, 0, 0)),
        compiler_params=pltpu.CompilerParams(vmem_limit_bytes=32 * 1024 * 1024),
        cost_estimate=pl.CostEstimate(
            flops=4 * CH_DEV * inputs * inputs * 2 * HALF * halves,
            bytes_accessed=3 * CH_DEV * inputs * inputs,
            transcendentals=0,
        ),
        name="correlate",
    )(pick, spectra)


def solution(mesh):
    placed = (P(None, ("band", "narrow", "wide"), None), P(), P(("band", "narrow", "wide")), P())
    return jax.shard_map(
        body,
        mesh=mesh,
        in_specs=placed,
        out_specs=P(("band", "wide"), None, "narrow", None),
        check_vma=False,
    )
```

time: 48.2 us -> 49.3 us (1.023)
  local copies, waits for them, and re-layouts: 1.59 us -> 2.63 us
    unnamed x4, local copies, waits for them, and re-layouts: 1.59 us -> 2.63 us
where the time goes in v2:
time: 49.3 us; the launch traced here: 49 us
  Pallas kernels  46.4 us (94%)
  local copies, waits for them, and re-layouts  2.63 us (5%)
    pallas_call x1, Pallas kernels, body(): pl.pallas_call(functools.partial(channelise, wide, nq, rows, halves), out...  39.6 us
    pallas_call x1, Pallas kernels, body(): pl.pallas_call(functools.partial(correlate, halves), grid=(CH_DEV,), out_...  6.81 us
    unnamed x4, local copies, waits for them, and re-layouts  2.63 us

profile of v2, /device:TPU:0, one launch (start us, length us, event | category | flops | bytes accessed | tf_op | source)
XLA Modules:
  0.0 49.0 jit_solution(8205245842345355222)
XLA Ops:
  0.0 39.6 %channelise.1 = (bf16[2,8,32,16,128]{4,3,2,1,0:T(8,128)(2,1)}, bf16[512,512]{1,0:T(8,128)(2,1)}) custom-call(bf16[2,32,268288]{2,1,0:T(8,128)(2,1)} %volt.1, bf16[2,4096,128]{2,1,0:T(8,128)(2,1)} %constant.2.clone.dft, f32[4,2048]{1,0:T(4,128)} %fir.1, s32[32]{0:T(128)} %flags.1, s32[1,256]{1,0:T(1,128)} %bitcast.1), custom_call_target="tpu_custom_call" | custom-call | flops 17985175552 | bytes 34340864 | tf_op jit(solution)/shard_map/channelise/pallas_call | solution.py:266
  39.6 0.0 copy-start
  39.6 1.6 %copy-done = bf16[2,8,32,16,128]{4,3,2,1,0:T(8,128)(2,1)S(1)} copy-done((bf16[2,8,32,16,128]{4,3,2,1,0:T(8,128)(2,1)S(1)}, bf16[2,8,32,16,128]{4,3,2,1,0:T(8,128)(2,1)}, u32[]{:S(2)}) %copy-start) | copy-done | bytes 2097176
  41.2 0.0 copy-start.1
  41.2 1.0 %copy-done.1 = bf16[512,512]{1,0:T(8,128)(2,1)S(1)} copy-done((bf16[512,512]{1,0:T(8,128)(2,1)S(1)}, bf16[512,512]{1,0:T(8,128)(2,1)}, u32[]{:S(2)}) %copy-start.1) | copy-done | bytes 524312
  42.2 6.8 %correlate.1 = bf16[8,2,256,512]{3,2,1,0:T(8,128)(2,1)} custom-call(bf16[512,512]{1,0:T(8,128)(2,1)S(1)} %copy-done.1, bf16[2,8,32,16,128]{4,3,2,1,0:T(8,128)(2,1)S(1)} %copy-done), custom_call_target="tpu_custom_call" | custom-call | flops 2147483648 | bytes 6291456 | tf_op jit(solution)/shard_map/correlate/pallas_call | solution.py:300
Async XLA Ops:
  39.6 1.6 %copy-start = (bf16[2,8,32,16,128]{4,3,2,1,0:T(8,128)(2,1)S(1)}, bf16[2,8,32,16,128]{4,3,2,1,0:T(8,128)(2,1)}, u32[]{:S(2)}) copy-start(bf16[2,8,32,16,128]{4,3,2,1,0:T(8,128)(2,1)} %get-tuple-element.8.spectra) | copy-start | bytes 6291460
  41.2 1.0 %copy-start.1 = (bf16[512,512]{1,0:T(8,128)(2,1)S(1)}, bf16[512,512]{1,0:T(8,128)(2,1)}, u32[]{:S(2)}) copy-start(bf16[512,512]{1,0:T(8,128)(2,1)} %get-tuple-element.7.pick) | copy-start | bytes 1572868

commit v3 on v1

--- a/solution.py
+++ b/solution.py
@@ -13,6 +13,7 @@
 NFFT = 2048
 TAPS = 4
 CH_DEV = 8
+CH_STEP = 4
 HALF = 64
 MESH = pl.DeviceIdType.MESH
 
@@ -26,7 +27,21 @@
     return np.concatenate([upper, lower], 0).astype(ml_dtypes.bfloat16)
 
 
-def channelise(wide, nq, rows, halves, volt, dft, fir, flags, out, frames, table, grid_sum, spec,
+def one_hot(order, inputs):
+    stations = inputs // 2
+    spread = (
+        lax.broadcasted_iota(jnp.int32, (stations, inputs), 0)
+        == lax.broadcasted_iota(jnp.int32, (stations, inputs), 1) // 2
+    ).astype(jnp.float32).astype(jnp.bfloat16)
+    row = jnp.broadcast_to(order.astype(jnp.float32), (16, stations)).astype(jnp.bfloat16)
+    wide_row = jnp.dot(row, spread, preferred_element_type=jnp.float32)[0:1]
+    odd = lax.broadcasted_iota(jnp.int32, (1, inputs), 1) % 2
+    column = 2 * wide_row.astype(jnp.int32) + odd
+    hit = lax.broadcasted_iota(jnp.int32, (inputs, inputs), 0) == column
+    return hit.astype(jnp.float32).T.astype(jnp.bfloat16)
+
+
+def channelise(wide, nq, rows, halves, volt, dft, fir, flags, order, out, pick, frames, table, grid_sum, spec,
                stage, send, in_sem, send_sem, recv_sem, own_sem, fwd_send, fwd_recv):
     me = lax.axis_index("wide")
     core = lax.axis_index("narrow")
@@ -38,8 +53,7 @@
     def load(chunk):
         q, th = chunk // halves, chunk % halves
 
-        @pl.loop(0, steps)
-        def _(s):
+        for s in range(steps):
             for part in range(2):
                 pltpu.make_async_copy(
                     volt.at[part, pl.ds(q * rows, rows), pl.ds(pl.multiple_of((th * HALF + s) * NFFT, NFFT), NFFT)],
@@ -47,14 +61,12 @@
                     in_sem.at[chunk],
                 ).start()
 
-    for chunk in range(chunks):
-        load(chunk)
-
     barrier = pltpu.get_barrier_semaphore()
     for d in range(1, wide):
         pl.semaphore_signal(barrier, inc=1, device_id={"wide": lax.rem(me + d, wide)}, device_id_type=MESH)
     pl.semaphore_signal(barrier, inc=1, device_id={"narrow": 1 - core}, device_id_type=MESH)
 
+    load(0)
     taps = jnp.concatenate([fir[...], fir[...]], 0).T
     step_n = 256
     for n0 in range(0, NFFT, step_n):
@@ -84,6 +96,10 @@
 
     @pl.loop(0, chunks)
     def _(chunk):
+        @pl.when(chunk + 1 < chunks)
+        def _():
+            load(chunk + 1)
+
         pltpu.make_async_copy(frames.at[chunk], frames.at[chunk], in_sem.at[chunk]).wait()
         lhs = frames[chunk]
         if rows % 16:
@@ -125,6 +141,8 @@
             device_id_type=MESH,
         ).start()
 
+    pick[...] = one_hot(order[...], pick.shape[0])
+
     @pl.loop(0, chunks)
     def _(chunk):
         for d in range(1, wide):
@@ -149,45 +167,33 @@
     pltpu.make_async_copy(own, own, own_sem).wait()
 
 
-def correlate(halves, order, spectra, out, pick):
-    inputs = pick.shape[0]
-    local = inputs // 2
+def flat(block):
+    count = block.shape[0] * block.shape[1]
+    if block.shape[1] % 16:
+        return block.astype(jnp.float32).reshape(count, 2 * HALF).astype(jnp.bfloat16)
+    return block.reshape(count, 2 * HALF)
+
+
+def correlate(halves, pick, spectra, out):
+    mine = spectra.shape[2] // 2
     core = lax.axis_index("narrow")
-
-    @pl.when(pl.program_id(0) == 0)
-    def _():
-        stations = inputs // 2
-        spread = (
-            lax.broadcasted_iota(jnp.int32, (stations, inputs), 0)
-            == lax.broadcasted_iota(jnp.int32, (stations, inputs), 1) // 2
-        ).astype(jnp.float32).astype(jnp.bfloat16)
-        row = jnp.broadcast_to(order[...].astype(jnp.float32), (16, stations)).astype(jnp.bfloat16)
-        wide_row = jnp.dot(row, spread, preferred_element_type=jnp.float32)[0:1]
-        odd = lax.broadcasted_iota(jnp.int32, (1, inputs), 1) % 2
-        column = 2 * wide_row.astype(jnp.int32) + odd
-        hit = lax.broadcasted_iota(jnp.int32, (inputs, inputs), 0) == column
-        pick[...] = hit.astype(jnp.float32).T.astype(jnp.bfloat16)
-
-    lane = lax.broadcasted_iota(jnp.int32, (inputs, 2 * HALF), 1)
-    sign = jnp.where(lane < HALF, -1.0, 1.0)
-    rows, cols, turned = [], [], []
-    for th in range(halves):
-        block = spectra[th, 0]
-        if block.shape[1] % 16:
-            block = block.astype(jnp.float32).reshape(inputs, 2 * HALF).astype(jnp.bfloat16)
-        else:
-            block = block.reshape(inputs, 2 * HALF)
-        rows.append(jnp.where(core == 0, block[:local], block[local:]))
+    contract = (((1,), (1,)), ((), ()))
+    for c in range(out.shape[0]):
+        block = jnp.concatenate([flat(spectra[th, c]) for th in range(halves)], 1)
+        left = jnp.concatenate(
+            [flat(spectra[th, c, pl.ds(core * mine, mine)]) for th in range(halves)], 1
+        )
         picked = jnp.dot(pick[...], block, preferred_element_type=jnp.float32)
-        cols.append(picked.astype(jnp.bfloat16))
-        turned.append((pltpu.roll(picked, HALF, 1) * sign).astype(jnp.bfloat16))
-    left = jnp.concatenate(rows, 1)
-    contract = (((1,), (1,)), ((), ()))
-    for part, right in enumerate((cols, turned)):
-        tile = lax.dot_general(
-            left, jnp.concatenate(right, 1), contract, preferred_element_type=jnp.float32
+        lane = lax.broadcasted_iota(jnp.int32, (picked.shape[0], 2 * HALF), 1)
+        sign = jnp.where(lane < HALF, -1.0, 1.0)
+        turned = jnp.concatenate(
+            [pltpu.roll(picked[:, b * 128 : (b + 1) * 128], HALF, 1) * sign for b in range(halves)], 1
         )
-        out[0, part] = (tile * (1.0 / (halves * HALF))).astype(jnp.bfloat16)
+        for part, right in enumerate((picked, turned)):
+            tile = lax.dot_general(
+                left, right.astype(jnp.bfloat16), contract, preferred_element_type=jnp.float32
+            )
+            out[c, part] = (tile * (1.0 / (halves * HALF))).astype(jnp.bfloat16)
 
 
 def body(voltages, fir_taps, flags, tile_order):
@@ -206,11 +212,14 @@
     inputs = groups * rows
     vmem = pl.BlockSpec(memory_space=pltpu.VMEM)
     hbm = pl.BlockSpec(memory_space=pl.ANY)
-    spectra = pl.pallas_call(
+    spectra, pick = pl.pallas_call(
         functools.partial(channelise, wide, nq, rows, halves),
-        out_shape=jax.ShapeDtypeStruct((halves, CH_DEV, groups, rows, 2 * HALF), jnp.bfloat16),
-        in_specs=[hbm, vmem, vmem, pl.BlockSpec(memory_space=pltpu.SMEM)],
-        out_specs=hbm,
+        out_shape=(
+            jax.ShapeDtypeStruct((halves, CH_DEV, groups, rows, 2 * HALF), jnp.bfloat16),
+            jax.ShapeDtypeStruct((inputs, inputs), jnp.bfloat16),
+        ),
+        in_specs=[hbm, vmem, vmem, pl.BlockSpec(memory_space=pltpu.SMEM), vmem],
+        out_specs=(hbm, vmem),
         scratch_shapes=[
             pltpu.VMEM((chunks, steps, rows, 2 * NFFT), jnp.bfloat16),
             pltpu.VMEM((2 * NFFT, TAPS * span), jnp.bfloat16),
@@ -234,25 +243,24 @@
             transcendentals=0,
         ),
         name="channelise",
-    )(voltages, jnp.asarray(dft_table(NFFT, kept)), fir_taps, flags)
+    )(voltages, jnp.asarray(dft_table(NFFT, kept)), fir_taps, flags, tile_order.reshape(1, -1))
     return pl.pallas_call(
         functools.partial(correlate, halves),
-        grid=(CH_DEV,),
+        grid=(CH_DEV // CH_STEP,),
         out_shape=jax.ShapeDtypeStruct((CH_DEV, 2, inputs // narrow, inputs), jnp.bfloat16),
         in_specs=[
-            pl.BlockSpec((1, tile_order.shape[0]), lambda c: (0, 0)),
-            pl.BlockSpec((halves, 1, groups, rows, 2 * HALF), lambda c: (0, c, 0, 0, 0)),
+            pl.BlockSpec((inputs, inputs), lambda c: (0, 0)),
+            pl.BlockSpec((halves, CH_STEP, groups, rows, 2 * HALF), lambda c: (0, c, 0, 0, 0)),
         ],
-        out_specs=pl.BlockSpec((1, 2, inputs // narrow, inputs), lambda c: (c, 0, 0, 0)),
-        scratch_shapes=[pltpu.VMEM((inputs, inputs), jnp.bfloat16)],
-        compiler_params=pltpu.CompilerParams(vmem_limit_bytes=32 * 1024 * 1024),
+        out_specs=pl.BlockSpec((CH_STEP, 2, inputs // narrow, inputs), lambda c: (c, 0, 0, 0)),
+        compiler_params=pltpu.CompilerParams(vmem_limit_bytes=60 * 1024 * 1024),
         cost_estimate=pl.CostEstimate(
             flops=4 * CH_DEV * inputs * inputs * 2 * HALF * halves,
             bytes_accessed=3 * CH_DEV * inputs * inputs,
             transcendentals=0,
         ),
         name="correlate",
-    )(tile_order.reshape(1, -1), spectra)
+    )(pick, spectra)
 
 
 def solution(mesh):

time: 48.2 us -> 45.3 us (0.940)
  local copies, waits for them, and re-layouts: 1.59 us -> 0 us
  Pallas kernels: 46.4 us -> 45.2 us
    unnamed x4 -> x0, local copies, waits for them, and re-layouts: 1.59 us -> none
    pallas_call x1, Pallas kernels: 7.2 us -> 5.82 us  [body(): pl.pallas_call(functools.partial(correlate, halves), grid=(CH_DEV // CH_S...]
where the time goes in v3:
time: 45.3 us; the launch traced here: 45.2 us
  Pallas kernels  45.2 us (100%)
    pallas_call x1, Pallas kernels, body(): pl.pallas_call(functools.partial(channelise, wide, nq, rows, halves), out...  39.3 us
    pallas_call x1, Pallas kernels, body(): pl.pallas_call(functools.partial(correlate, halves), grid=(CH_DEV // CH_S...  5.82 us

profile of v3, /device:TPU:0, one launch (start us, length us, event | category | flops | bytes accessed | tf_op | source)
XLA Modules:
  0.0 45.2 jit_solution(718241782386074686)
XLA Ops:
  0.0 39.3 %channelise.1 = (bf16[2,8,32,16,128]{4,3,2,1,0:T(8,128)(2,1)}, bf16[512,512]{1,0:T(8,128)(2,1)}) custom-call(bf16[2,32,268288]{2,1,0:T(8,128)(2,1)} %volt.1, bf16[4096,128]{1,0:T(8,128)(2,1)} %constant.2.clone.dft, f32[4,2048]{1,0:T(4,128)} %fir.1, s32[32]{0:T(128)} %flags.1, s32[1,256]{1,0:T(1,128)} %bitcast.1), custom_call_target="tpu_custom_call" | custom-call | flops 17985175552 | bytes 34340864 | tf_op jit(solution)/shard_map/channelise/pallas_call | solution.py:215
  39.4 5.8 %correlate.1 = bf16[8,2,256,512]{3,2,1,0:T(8,128)(2,1)} custom-call(bf16[512,512]{1,0:T(8,128)(2,1)} %get-tuple-element.7.pick, bf16[2,8,32,16,128]{4,3,2,1,0:T(8,128)(2,1)} %get-tuple-element.8.spectra), custom_call_target="tpu_custom_call" | custom-call | flops 2147483648 | bytes 6291456 | tf_op jit(solution)/shard_map/correlate/pallas_call | solution.py:247

commit v4 on v3

--- a/solution.py
+++ b/solution.py
@@ -14,6 +14,7 @@
 TAPS = 4
 CH_DEV = 8
 CH_STEP = 4
+SPLIT = [0, 34]
 HALF = 64
 MESH = pl.DeviceIdType.MESH
 
@@ -49,6 +50,7 @@
     span = 2 * kept
     steps = HALF + TAPS - 1
     chunks = nq * halves
+    split = SPLIT
 
     def load(chunk):
         q, th = chunk // halves, chunk % halves
@@ -58,7 +60,7 @@
                 pltpu.make_async_copy(
                     volt.at[part, pl.ds(q * rows, rows), pl.ds(pl.multiple_of((th * HALF + s) * NFFT, NFFT), NFFT)],
                     frames.at[chunk, s, :, pl.ds(part * NFFT, NFFT)],
-                    in_sem.at[chunk],
+                    in_sem.at[chunk, split.index(max(x for x in split if x <= s))],
                 ).start()
 
     barrier = pltpu.get_barrier_semaphore()
@@ -100,13 +102,18 @@
         def _():
             load(chunk + 1)
 
-        pltpu.make_async_copy(frames.at[chunk], frames.at[chunk], in_sem.at[chunk]).wait()
-        lhs = frames[chunk]
-        if rows % 16:
-            lhs = lhs.astype(jnp.float32).reshape(steps * rows, 2 * NFFT).astype(jnp.bfloat16)
-        else:
-            lhs = lhs.reshape(steps * rows, 2 * NFFT)
-        grid_sum[...] = jnp.dot(lhs, table[...], preferred_element_type=jnp.float32)
+        for b, first in enumerate(split):
+            last = (split + [steps])[b + 1]
+            here = frames.at[chunk, pl.ds(first, last - first)]
+            pltpu.make_async_copy(here, here, in_sem.at[chunk, b]).wait()
+            lhs = frames[chunk, first:last]
+            if rows % 16:
+                lhs = lhs.astype(jnp.float32).reshape((last - first) * rows, 2 * NFFT).astype(jnp.bfloat16)
+            else:
+                lhs = lhs.reshape((last - first) * rows, 2 * NFFT)
+            grid_sum[first * rows : last * rows] = jnp.dot(
+                lhs, table[...], preferred_element_type=jnp.float32
+            )
         count = HALF * rows
         total = grid_sum[0:count, 0:span]
         for k in range(1, TAPS):
@@ -227,7 +234,7 @@
             pltpu.VMEM((span // 128, HALF * rows, 128), jnp.float32),
             pltpu.VMEM((kept * rows, 2 * HALF), jnp.float32),
             pltpu.VMEM((chunks, kept, rows, 2 * HALF), jnp.bfloat16),
-            pltpu.SemaphoreType.DMA((chunks,)),
+            pltpu.SemaphoreType.DMA((chunks, len(SPLIT))),
             pltpu.SemaphoreType.DMA,
             pltpu.SemaphoreType.DMA((chunks, wide)),
             pltpu.SemaphoreType.DMA,

time: 45.3 us -> 44.2 us (0.976)
  Pallas kernels: 45.2 us -> 44 us
    pallas_call x1, Pallas kernels: 39.3 us -> 38.2 us  [body(): pl.pallas_call(functools.partial(channelise, wide, nq, rows, halves), out...]
where the time goes in v4:
time: 44.2 us; the launch traced here: 44 us
  Pallas kernels  44 us (100%)
    pallas_call x1, Pallas kernels, body(): pl.pallas_call(functools.partial(channelise, wide, nq, rows, halves), out...  38.2 us
    pallas_call x1, Pallas kernels, body(): pl.pallas_call(functools.partial(correlate, halves), grid=(CH_DEV // CH_S...  5.82 us

profile of v4, /device:TPU:0, one launch (start us, length us, event | category | flops | bytes accessed | tf_op | source)
XLA Modules:
  0.0 44.0 jit_solution(9244937356675872335)
XLA Ops:
  0.0 38.2 %channelise.1 = (bf16[2,8,32,16,128]{4,3,2,1,0:T(8,128)(2,1)}, bf16[512,512]{1,0:T(8,128)(2,1)}) custom-call(bf16[2,32,268288]{2,1,0:T(8,128)(2,1)} %volt.1, bf16[4096,128]{1,0:T(8,128)(2,1)} %constant.2.clone.dft, f32[4,2048]{1,0:T(4,128)} %fir.1, s32[32]{0:T(128)} %flags.1, s32[1,256]{1,0:T(1,128)} %bitcast.1), custom_call_target="tpu_custom_call" | custom-call | flops 17985175552 | bytes 34340864 | tf_op jit(solution)/shard_map/channelise/pallas_call | solution.py:222
  38.2 5.8 %correlate.1 = bf16[8,2,256,512]{3,2,1,0:T(8,128)(2,1)} custom-call(bf16[512,512]{1,0:T(8,128)(2,1)} %get-tuple-element.7.pick, bf16[2,8,32,16,128]{4,3,2,1,0:T(8,128)(2,1)} %get-tuple-element.8.spectra), custom_call_target="tpu_custom_call" | custom-call | flops 2147483648 | bytes 6291456 | tf_op jit(solution)/shard_map/correlate/pallas_call | solution.py:254
